TPU v7x, 256 devices: a whole 4x4x8 slice. The times are simulated.
256 devices in a mesh: dx: 32 (over z, x_lo, core), dy: 8 (over x_hi, y).
Axes of the slice: x: 4 (x_hi: 2, x_lo: 2; x = x_hi * 2 + x_lo), y: 4, z: 8, core: 2. Of those that a mesh axis runs over, the one named last changes fastest.
Arguments:
- img_emb: bfloat16 [131072, 1152], P(('dx', 'dy')), may hold values from -0.1796875 to 0.1796875
- txt_emb: bfloat16 [131072, 1152], P(('dx', 'dy')), may hold values from -0.1796875 to 0.1796875
- logit_scale: float32 [1], replicated, may hold values from 4 to 8
- logit_bias: float32 [1], replicated, may hold values from -3 to -1
Outputs:
- grad_img: float32 [131072, 1152], P(('dx', 'dy'))
- grad_txt: float32 [131072, 1152], P(('dx', 'dy'))
All inputs are finite; a program needn't handle non-finite values.
Results may differ from a plain program's by a relative error of at most 0.0049.
Values may be sent and summed in bfloat16 or wider, within the bound.
A program may use at most 64 MiB of HBM per device.

v0:
```python
import jax
import jax.numpy as jnp
from jax import lax
from jax.sharding import PartitionSpec as P


def from_partner(value, axis, stride):
    return lax.ppermute(value, axis, [(i, i ^ 1 << stride) for i in range(lax.axis_size(axis))])


def normalize(values):
    floats = values.astype(jnp.float32)
    inverse = lax.rsqrt(jnp.sum(floats * floats, axis=-1, keepdims=True) + 1e-06)
    return (floats * inverse, inverse)


def tile_weights(images, texts, scale, bias, diagonal):
    logits = (
        scale
        * lax.dot_general(
            images, texts, (((1,), (1,)), ((), ())), preferred_element_type=jnp.float32
        )
        + bias
    )
    if diagonal:
        eye = jnp.arange(images.shape[0])[:, None] == jnp.arange(texts.shape[0])[None, :]
        signs = jnp.where(eye, jnp.float32(1.0), jnp.float32(-1.0))
    else:
        signs = jnp.full(logits.shape, -1.0, jnp.float32)
    coeffs = -signs * jax.nn.sigmoid(-signs * logits)
    return (scale * coeffs).astype(jnp.bfloat16)


def transposed(coeffs, images):
    return lax.dot_general(
        coeffs, images, (((0,), (0,)), ((), ())), preferred_element_type=jnp.float32
    )


def finish(unit, inverse, grads):
    return inverse * (grads - unit * jnp.sum(unit * grads, axis=-1, keepdims=True))


def per_device(img_emb, txt_emb, logit_scale, logit_bias):
    img_unit, inv_img = normalize(img_emb)
    txt_unit, inv_txt = normalize(txt_emb)
    img_b = img_unit.astype(jnp.bfloat16)
    txt_b = txt_unit.astype(jnp.bfloat16)
    scale = logit_scale[0]
    bias = logit_bias[0]
    own_coeffs = tile_weights(img_b, txt_b, scale, bias, True)
    grad_i = jnp.dot(own_coeffs, txt_b, preferred_element_type=jnp.float32)
    grad_t = transposed(own_coeffs, img_b)
    top_bit = lax.axis_size("dx").bit_length() - 2

    def forward_part(far_txt):
        coeffs = tile_weights(img_b, far_txt, scale, bias, False)
        more = jnp.dot(coeffs, far_txt, preferred_element_type=jnp.float32)
        return (more, transposed(coeffs, img_b).astype(jnp.bfloat16))

    far_txt = from_partner(txt_b, "dy", 0)
    more, partial_value = forward_part(far_txt)
    grad_i = grad_i + more
    grad_t = grad_t + from_partner(partial_value, "dy", 0).astype(jnp.float32)
    for bit_index in (0, top_bit, 1):
        far_txt = from_partner(txt_b, "dx", bit_index)
        more, partial_value = forward_part(far_txt)
        grad_i = grad_i + more
        grad_t = grad_t + from_partner(partial_value, "dx", bit_index).astype(jnp.float32)
    return (finish(img_unit, inv_img, grad_i), finish(txt_unit, inv_txt, grad_t))


def solution(mesh):
    return jax.shard_map(
        per_device,
        mesh=mesh,
        in_specs=(P(("dx", "dy"), None), P(("dx", "dy"), None), P(), P()),
        out_specs=(P(("dx", "dy"), None), P(("dx", "dy"), None)),
        check_vma=False,
    )
```

profile of v0, /device:TPU:38, one launch (start us, length us, event | category | flops | bytes accessed | tf_op | source)
XLA Modules:
  0.0 120.7 jit_solution(6003044242232505073)
XLA Ops:
  0.6 1.7 %fusion.15 = f32[512]{0:T(512)S(1)} fusion(bf16[512,1152]{1,0:T(8,128)(2,1)} %param.5), kind=kLoop, calls=%fused_computation.25 | loop fusion | flops 1768960 | bytes 1181696 | tf_op jit(solution)/shard_map/reduce_sum | solution.py:13
  2.6 0.9 collective-permute-start.3
  3.5 6.3 %collective-permute-start.2 = (bf16[512,1152]{1,0:T(8,128)(2,1)S(1)}, bf16[512,1152]{1,0:T(8,128)(2,1)S(1)}, u32[]{:S(2)}, u32[]{:S(2)}) collective-permute-start(bf16[512,1152]{1,0:T(8,128)(2,1)S(1)} %fusion.4), channel_id=1, source_target_pairs={{0,128},{8,136},{16,144},{24,152},{32,160},{40,168},{48,176},{56,1... | collective-permute-start | bytes 3538952 | tf_op jit(solution)/shard_map/ppermute | solution.py:8
  9.8 1.6 %collective-permute-start = (bf16[512,1152]{1,0:T(8,128)(2,1)S(1)}, bf16[512,1152]{1,0:T(8,128)(2,1)S(1)}, u32[]{:S(2)}, u32[]{:S(2)}) collective-permute-start(bf16[512,1152]{1,0:T(8,128)(2,1)S(1)} %fusion.4), channel_id=1, source_target_pairs={{0,1},{1,0},{2,3},{3,2},{4,5},{5,4},{6,7},{7,6},{8,9},{9,8},{10,11... | collective-permute-start | bytes 3538952 | tf_op jit(solution)/shard_map/ppermute | solution.py:8
  13.0 1.1 fusion.48
  15.0 15.4 %collective-permute-done.3 = bf16[512,1152]{1,0:T(8,128)(2,1)S(1)} collective-permute-done((bf16[512,1152]{1,0:T(8,128)(2,1)S(1)}, bf16[512,1152]{1,0:T(8,128)(2,1)S(1)}, u32[]{:S(2)}, u32[]{:S(2)}) %collective-permute-start.3) | collective-permute-done | bytes 1179680 | tf_op jit(solution)/shard_map/ppermute | solution.py:8
  30.4 1.0 fusion.49
  31.5 0.9 convolution_convert_fusion
  32.4 0.9 collective-permute-start.7
  33.4 27.7 %collective-permute-done.2 = bf16[512,1152]{1,0:T(8,128)(2,1)S(1)} collective-permute-done((bf16[512,1152]{1,0:T(8,128)(2,1)S(1)}, bf16[512,1152]{1,0:T(8,128)(2,1)S(1)}, u32[]{:S(2)}, u32[]{:S(2)}) %collective-permute-start.2) | collective-permute-done | bytes 1179680 | tf_op jit(solution)/shard_map/ppermute | solution.py:8
  61.1 1.1 fusion.50
  62.1 0.9 convolution_convert_fusion.1
  63.1 5.6 %collective-permute-start.6 = (bf16[512,1152]{1,0:T(8,128)(2,1)S(1)}, bf16[512,1152]{1,0:T(8,128)(2,1)S(1)}, u32[]{:S(2)}, u32[]{:S(2)}) collective-permute-start(bf16[512,1152]{1,0:T(8,128)(2,1)S(1)} %convolution_convert_fusion.1), channel_id=1, source_target_pairs={{0,128},{8,136},{16,144},{24,152},{32,160},{40,168},{48,176},{56,1... | collective-permute-start | bytes 3538952 | tf_op jit(solution)/shard_map/ppermute | solution.py:8
  68.7 1.1 fusion.51
  69.8 1.0 convolution_convert_fusion.2
  71.0 1.1 fusion.52
  72.1 1.0 convolution_convert_fusion.3
  73.1 1.7 %collective-permute-start.4 = (bf16[512,1152]{1,0:T(8,128)(2,1)S(1)}, bf16[512,1152]{1,0:T(8,128)(2,1)S(1)}, u32[]{:S(2)}, u32[]{:S(2)}) collective-permute-start(bf16[512,1152]{1,0:T(8,128)(2,1)S(1)} %convolution_convert_fusion.3), channel_id=1, source_target_pairs={{0,1},{1,0},{2,3},{3,2},{4,5},{5,4},{6,7},{7,6},{8,9},{9,8},{10,11... | collective-permute-start | bytes 3538952 | tf_op jit(solution)/shard_map/ppermute | solution.py:8
  76.4 0.8 convolution_add_fusion.1
  77.3 1.3 %fusion.8 = (f32[512]{0:T(512)S(1)}, f32[512,1152]{1,0:T(8,128)S(1)}) fusion(bf16[512,1152]{1,0:T(8,128)(2,1)S(1)} %copy-done.1, f32[512]{0:T(512)S(1)} %add_rsqrt_fusion.1, f32[512,1152]{1,0:T(8,128)S(1)} %fusion.66, f32[512,1152]{1,0:T(8,128)S(1)} %fusion.65, f32[512,1152]{1,0:T(8,128)S(1)} %convolution_add_fusion.1, bf16[512,512]{1,0:T(8,128)(2,1)S(1)} %fusion.51, ...), kind=kOutput, calls=%fused_computation.18 | convolution fusion | flops 608108032 | bytes 12324864 | tf_op jit(solution)/shard_map/dot_general | solution.py:58
  78.5 1.9 %fusion.10 = f32[512,1152]{1,0:T(8,128)} fusion(f32[512,1152]{1,0:T(8,128)S(1)} %get-tuple-element.3, bf16[512,1152]{1,0:T(8,128)(2,1)S(1)} %copy-done.1, f32[512]{0:T(512)S(1)} %get-tuple-element.2, f32[512]{0:T(512)S(1)} %add_rsqrt_fusion.1), kind=kLoop, calls=%fused_computation.20 | loop fusion | flops 2949120 | bytes 5902336 | tf_op jit(solution)/shard_map/mul | solution.py:41
  80.4 36.1 %collective-permute-done.6 = bf16[512,1152]{1,0:T(8,128)(2,1)S(1)} collective-permute-done((bf16[512,1152]{1,0:T(8,128)(2,1)S(1)}, bf16[512,1152]{1,0:T(8,128)(2,1)S(1)}, u32[]{:S(2)}, u32[]{:S(2)}) %collective-permute-start.6) | collective-permute-done | bytes 1179680 | tf_op jit(solution)/shard_map/ppermute | solution.py:8
  116.5 1.8 %fusion.12 = (f32[512]{0:T(512)S(1)}, f32[512,1152]{1,0:T(8,128)S(1)}) fusion(bf16[512,1152]{1,0:T(8,128)(2,1)S(1)} %copy-done, f32[512]{0:T(512)S(1)} %add_rsqrt_fusion, bf16[512,1152]{1,0:T(8,128)(2,1)S(1)} %collective-permute-done.7, bf16[512,1152]{1,0:T(8,128)(2,1)S(1)} %collective-permute-done.6, bf16[512,1152]{1,0:T(8,128)(2,1)S(1)} %collective-permute-done.5, ...), kind=kOutput, calls=%fused_computation.22 | convolution fusion | flops 612826624 | bytes 9967616 | tf_op jit(solution)/shard_map/dot_general | solution.py:35
  118.3 2.4 %fusion.14 = f32[512,1152]{1,0:T(8,128)} fusion(bf16[512,1152]{1,0:T(8,128)(2,1)S(1)} %copy-done, f32[512]{0:T(512)S(1)} %get-tuple-element.4, f32[512]{0:T(512)S(1)} %add_rsqrt_fusion, bf16[512,1152]{1,0:T(8,128)(2,1)S(1)} %collective-permute-done.7, bf16[512,1152]{1,0:T(8,128)(2,1)S(1)} %collective-permute-done.6, ...), kind=kLoop, calls=%fused_computation.24 | loop fusion | flops 7667712 | bytes 10620928 | tf_op jit(solution)/shard_map/mul | solution.py:41
  (18 shorter events, 3.4 us)
Async XLA Ops:
  0.6 1.7 %copy-start = (bf16[512,1152]{1,0:T(8,128)(2,1)S(1)}, bf16[512,1152]{1,0:T(8,128)(2,1)}, u32[]{:S(2)}) copy-start(bf16[512,1152]{1,0:T(8,128)(2,1)} %param.5) | copy-start | bytes 3538948
  2.3 10.4 %copy-start.1 = (bf16[512,1152]{1,0:T(8,128)(2,1)S(1)}, bf16[512,1152]{1,0:T(8,128)(2,1)}, u32[]{:S(2)}) copy-start(bf16[512,1152]{1,0:T(8,128)(2,1)} %param.4) | copy-start | bytes 3538948
  2.6 27.8 %collective-permute-start.3 = (bf16[512,1152]{1,0:T(8,128)(2,1)S(1)}, bf16[512,1152]{1,0:T(8,128)(2,1)S(1)}, u32[]{:S(2)}, u32[]{:S(2)}) collective-permute-start(bf16[512,1152]{1,0:T(8,128)(2,1)S(1)} %fusion.4), channel_id=1, source_target_pairs={{0,16},{8,24},{16,0},{24,8},{32,48},{40,56},{48,32},{56,40},{64,80... | collective-permute-start | bytes 3538952 | tf_op jit(solution)/shard_map/ppermute | solution.py:8
  3.5 57.6 %collective-permute-start.2 = (bf16[512,1152]{1,0:T(8,128)(2,1)S(1)}, bf16[512,1152]{1,0:T(8,128)(2,1)S(1)}, u32[]{:S(2)}, u32[]{:S(2)}) collective-permute-start(bf16[512,1152]{1,0:T(8,128)(2,1)S(1)} %fusion.4), channel_id=1, source_target_pairs={{0,128},{8,136},{16,144},{24,152},{32,160},{40,168},{48,176},{56,1... | collective-permute-start | bytes 3538952 | tf_op jit(solution)/shard_map/ppermute | solution.py:8
  9.8 61.2 %collective-permute-start = (bf16[512,1152]{1,0:T(8,128)(2,1)S(1)}, bf16[512,1152]{1,0:T(8,128)(2,1)S(1)}, u32[]{:S(2)}, u32[]{:S(2)}) collective-permute-start(bf16[512,1152]{1,0:T(8,128)(2,1)S(1)} %fusion.4), channel_id=1, source_target_pairs={{0,1},{1,0},{2,3},{3,2},{4,5},{5,4},{6,7},{7,6},{8,9},{9,8},{10,11... | collective-permute-start | bytes 3538952 | tf_op jit(solution)/shard_map/ppermute | solution.py:8
  11.4 57.3 %collective-permute-start.1 = (bf16[512,1152]{1,0:T(8,128)(2,1)S(1)}, bf16[512,1152]{1,0:T(8,128)(2,1)S(1)}, u32[]{:S(2)}, u32[]{:S(2)}) collective-permute-start(bf16[512,1152]{1,0:T(8,128)(2,1)S(1)} %fusion.4), channel_id=1, source_target_pairs={{0,8},{8,0},{16,24},{24,16},{32,40},{40,32},{48,56},{56,48},{64,72... | collective-permute-start | bytes 3538952 | tf_op jit(solution)/shard_map/ppermute | solution.py:8
  32.4 48.0 %collective-permute-start.7 = (bf16[512,1152]{1,0:T(8,128)(2,1)S(1)}, bf16[512,1152]{1,0:T(8,128)(2,1)S(1)}, u32[]{:S(2)}, u32[]{:S(2)}) collective-permute-start(bf16[512,1152]{1,0:T(8,128)(2,1)S(1)} %convolution_convert_fusion), channel_id=1, source_target_pairs={{0,16},{8,24},{16,0},{24,8},{32,48},{40,56},{48,32},{56,40},{64,80... | collective-permute-start | bytes 3538952 | tf_op jit(solution)/shard_map/ppermute | solution.py:8
  63.1 53.4 %collective-permute-start.6 = (bf16[512,1152]{1,0:T(8,128)(2,1)S(1)}, bf16[512,1152]{1,0:T(8,128)(2,1)S(1)}, u32[]{:S(2)}, u32[]{:S(2)}) collective-permute-start(bf16[512,1152]{1,0:T(8,128)(2,1)S(1)} %convolution_convert_fusion.1), channel_id=1, source_target_pairs={{0,128},{8,136},{16,144},{24,152},{32,160},{40,168},{48,176},{56,1... | collective-permute-start | bytes 3538952 | tf_op jit(solution)/shard_map/ppermute | solution.py:8
  70.7 45.8 %collective-permute-start.5 = (bf16[512,1152]{1,0:T(8,128)(2,1)S(1)}, bf16[512,1152]{1,0:T(8,128)(2,1)S(1)}, u32[]{:S(2)}, u32[]{:S(2)}) collective-permute-start(bf16[512,1152]{1,0:T(8,128)(2,1)S(1)} %convolution_convert_fusion.2), channel_id=1, source_target_pairs={{0,8},{8,0},{16,24},{24,16},{32,40},{40,32},{48,56},{56,48},{64,72... | collective-permute-start | bytes 3538952 | tf_op jit(solution)/shard_map/ppermute | solution.py:8
  73.1 43.5 %collective-permute-start.4 = (bf16[512,1152]{1,0:T(8,128)(2,1)S(1)}, bf16[512,1152]{1,0:T(8,128)(2,1)S(1)}, u32[]{:S(2)}, u32[]{:S(2)}) collective-permute-start(bf16[512,1152]{1,0:T(8,128)(2,1)S(1)} %convolution_convert_fusion.3), channel_id=1, source_target_pairs={{0,1},{1,0},{2,3},{3,2},{4,5},{5,4},{6,7},{7,6},{8,9},{9,8},{10,11... | collective-permute-start | bytes 3538952 | tf_op jit(solution)/shard_map/ppermute | solution.py:8
where the time goes:
time: 122 us; the launch traced here: 121 us
  waiting for transfers between devices  79.2 us (65%)
  starting transfers between devices  17.3 us (14%)
  matrix products  15.5 us (13%)
  other arithmetic  6.56 us (5%)
  between operations  2.08 us (2%)
    ppermute x8, waiting for transfers between devices, from_partner(): lax.ppermute(value, axis, [(i, i ^ 1 << stride) for i in range(lax.axis_s...  79.2 us
    ppermute x8, starting transfers between devices, from_partner(): lax.ppermute(value, axis, [(i, i ^ 1 << stride) for i in range(lax.axis_s...  17.3 us
    dot_general x5, matrix products, transposed(): lax.dot_general(coeffs, images, (((0,), (0,)), ((), ())), preferred_eleme...  5.56 us
    dot_general x5, matrix products, tile_weights(): lax.dot_general(images, texts, (((1,), (1,)), ((), ())), preferred_elemen...  5.32 us
    mul x2, other arithmetic, finish(): inverse * (grads - unit * jnp.sum(unit * grads, axis=-1, keepdims=True))  4.31 us
    dot_general x4, matrix products, forward_part(): more = jnp.dot(coeffs, far_txt, preferred_element_type=jnp.float32)  3.81 us
  transfers between devices with their start and end apart: 8, of which 3 were waited for; matrix products, arithmetic and copies ran while one was open for 13% of the time, Pallas kernels for 0%

commit v1 on v0

v1 whole, which is shorter than its diff:
```python
import functools

import jax
import jax.numpy as jnp
from jax import lax
from jax.experimental import pallas as pl
from jax.experimental.pallas import tpu as pltpu
from jax.sharding import PartitionSpec as P

ROWS = 512
E = 1152
STEP = 256
Z_ROWS = 128
FINISH_ROWS = 128
IMG, TXT = 0, 1
CORE, Y, X, Z = 0, 1, 2, 3


def flipped(index, bit):
    return jnp.where(lax.rem(index // bit, 2) == 1, index - bit, index + bit)


def projected(grads, raw, inverse):
    units = raw.astype(jnp.float32) * inverse
    return inverse * (grads - units * jnp.sum(units * grads, axis=-1, keepdims=True))


def unit_rows(values):
    floats = values.astype(jnp.float32)
    inverse = lax.rsqrt(jnp.sum(floats * floats, axis=-1, keepdims=True) + 1e-06)
    return floats * inverse, inverse


def gather_kernel(n_dx, img, txt, scale_ref, bias_ref, out_img, out_txt, raw, inv, unit, far,
                  load_sem, send_sem, recv_sem, z_send, z_recv):
    dx, dy = lax.axis_index("dx"), lax.axis_index("dy")
    partners = (
        (flipped(dx, 1), dy),
        (dx, flipped(dy, 1)),
        (flipped(dx, 2), dy),
        (flipped(dx, n_dx // 2), dy),
    )
    scale, bias = scale_ref[0], bias_ref[0]
    blocks = (img, txt)
    outs = (out_img, out_txt)

    loads = [pltpu.make_async_copy(blocks[kind], raw.at[kind], load_sem.at[kind]) for kind in (IMG, TXT)]
    for load in loads:
        load.start()

    barrier = pltpu.get_barrier_semaphore()
    for partner in partners:
        pl.semaphore_signal(barrier, inc=1, device_id=partner, device_id_type=pl.DeviceIdType.MESH)
    pl.semaphore_wait(barrier, 4)

    z_copies, copies = {}, {}
    per_kind = ROWS // Z_ROWS
    for kind in (TXT, IMG):
        for part in range(per_kind):
            rows = pl.ds(part * Z_ROWS, Z_ROWS)
            z_copies[kind, part] = pltpu.make_async_remote_copy(
                src_ref=blocks[kind].at[rows],
                dst_ref=far.at[Z, kind, rows],
                send_sem=z_send.at[kind, part],
                recv_sem=z_recv.at[kind, part],
                device_id=partners[Z],
                device_id_type=pl.DeviceIdType.MESH,
            )
    for kind in (TXT, IMG):
        for part in range(per_kind):
            z_copies[kind, part].start()
    for kind in (TXT, IMG):
        for way in (Y, X, CORE):
            copies[way, kind] = pltpu.make_async_remote_copy(
                src_ref=blocks[kind],
                dst_ref=far.at[way, kind],
                send_sem=send_sem.at[way, kind],
                recv_sem=recv_sem.at[way, kind],
                device_id=partners[way],
                device_id_type=pl.DeviceIdType.MESH,
            )
            copies[way, kind].start()

    for load in loads:
        load.wait()

    @pl.loop(0, ROWS // 128)
    def _(step):
        rows = pl.ds(step * 128, 128)
        for kind in (IMG, TXT):
            units, inverse = unit_rows(raw[kind, rows, :])
            unit[kind, rows, :] = units.astype(jnp.bfloat16)
            inv[kind, rows, :] = inverse

    def tile(kind, others, row, diagonal=None):
        mine = 1 - kind
        rows = pl.ds(row, STEP)
        logits = scale * lax.dot_general(
            unit[mine, rows, :], others, (((1,), (1,)), ((), ())), preferred_element_type=jnp.float32
        ) + bias
        if diagonal is None:
            coeffs = jax.nn.sigmoid(logits)
        else:
            first = row + lax.broadcasted_iota(jnp.int32, logits.shape, 0)
            second = diagonal + lax.broadcasted_iota(jnp.int32, logits.shape, 1)
            signs = jnp.where(first == second, jnp.float32(1.0), jnp.float32(-1.0))
            coeffs = -signs * jax.nn.sigmoid(-signs * logits)
        return jnp.dot((scale * coeffs).astype(jnp.bfloat16), others, preferred_element_type=jnp.float32)

    for kind in (TXT, IMG):
        mine = 1 - kind
        for row in range(0, ROWS, STEP):
            outs[mine][row : row + STEP, :] = tile(kind, unit[kind, 0:STEP, :], row, 0)
            outs[mine][row : row + STEP, :] += tile(kind, unit[kind, STEP:ROWS, :], row, STEP)

    def add_tiles(way, kind, start, count):
        mine = 1 - kind
        others = unit_rows(far[way, kind, pl.ds(start, count), :])[0].astype(jnp.bfloat16)
        for row in range(0, ROWS, STEP):
            outs[mine][row : row + STEP, :] += tile(kind, others, row)

    for way in (CORE, Y, X):
        for kind in (TXT, IMG):
            copies[way, kind].wait_recv()

            @pl.loop(0, ROWS // STEP)
            def _(step):
                add_tiles(way, kind, step * STEP, STEP)

    for kind in (TXT, IMG):
        for part in range(per_kind):
            z_copies[kind, part].wait_recv()
            add_tiles(Z, kind, part * Z_ROWS, Z_ROWS)
        if kind == TXT:

            @pl.loop(0, ROWS // 128)
            def _(step):
                rows = pl.ds(step * 128, 128)
                out_img[rows, :] = projected(out_img[rows, :], raw[IMG, rows, :], inv[IMG, rows, :])

    for copy in (*z_copies.values(), *copies.values()):
        copy.wait_send()


def finish_kernel(grad_img, sum_txt, raw, inv, out_img, out_txt, grad_txt, sem):
    whole = pltpu.make_async_copy(grad_img, out_img, sem.at[0])
    whole.start()
    parts = []
    for part in range(ROWS // FINISH_ROWS):
        rows = pl.ds(part * FINISH_ROWS, FINISH_ROWS)
        grad_txt[rows, :] = projected(sum_txt[rows, :], raw[TXT, rows, :], inv[TXT, rows, :])
        parts.append(pltpu.make_async_copy(grad_txt.at[rows], out_txt.at[rows], sem.at[1 + part]))
        parts[-1].start()
    for copy in (whole, *parts):
        copy.wait()


def per_device(n_dx, img_emb, txt_emb, logit_scale, logit_bias):
    per_kind = ROWS // Z_ROWS
    vmem = pl.BlockSpec(memory_space=pltpu.VMEM)
    img_emb = pltpu.with_memory_space_constraint(img_emb, pltpu.HBM)
    txt_emb = pltpu.with_memory_space_constraint(txt_emb, pltpu.HBM)
    sums = pl.pallas_call(
        functools.partial(gather_kernel, n_dx),
        out_shape=(
            pltpu.VMEM((ROWS, E), jnp.float32),
            pltpu.VMEM((ROWS, E), jnp.float32),
            pltpu.VMEM((2, ROWS, E), jnp.bfloat16),
            pltpu.VMEM((2, ROWS, 1), jnp.float32),
        ),
        in_specs=[pl.BlockSpec(memory_space=pltpu.HBM)] * 2 + [pl.BlockSpec(memory_space=pltpu.SMEM)] * 2,
        out_specs=[vmem] * 4,
        scratch_shapes=[
            pltpu.VMEM((2, ROWS, E), jnp.bfloat16),
            pltpu.VMEM((4, 2, ROWS, E), jnp.bfloat16),
            pltpu.SemaphoreType.DMA((2,)),
            pltpu.SemaphoreType.DMA((3, 2)),
            pltpu.SemaphoreType.DMA((3, 2)),
            pltpu.SemaphoreType.DMA((2, per_kind)),
            pltpu.SemaphoreType.DMA((2, per_kind)),
        ],
        compiler_params=pltpu.CompilerParams(
            collective_id=0, has_side_effects=True, vmem_limit_bytes=40 * 2**20
        ),
        name="window_sums",
    )(img_emb, txt_emb, logit_scale, logit_bias)
    out = jax.ShapeDtypeStruct((ROWS, E), jnp.float32)
    return pl.pallas_call(
        finish_kernel,
        out_shape=(out, out),
        in_specs=[vmem] * 4,
        out_specs=[pl.BlockSpec(memory_space=pl.ANY)] * 2,
        scratch_shapes=[
            pltpu.VMEM((ROWS, E), jnp.float32),
            pltpu.SemaphoreType.DMA((1 + ROWS // FINISH_ROWS,)),
        ],
        compiler_params=pltpu.CompilerParams(vmem_limit_bytes=40 * 2**20),
        name="window_finish",
    )(*(pltpu.with_memory_space_constraint(value, pltpu.VMEM) for value in sums))


def solution(mesh):
    return jax.shard_map(
        functools.partial(per_device, mesh.shape["dx"]),
        mesh=mesh,
        in_specs=(P(("dx", "dy"), None), P(("dx", "dy"), None), P(), P()),
        out_specs=(P(("dx", "dy"), None), P(("dx", "dy"), None)),
        check_vma=False,
    )
```

time: 122 us -> 116 us (0.951); the launches traced: 121 us -> 116 us
  Pallas kernels: 0 us -> 114 us
  waiting for transfers between devices: 79.2 us -> 0 us
  starting transfers between devices: 17.3 us -> 0 us
  matrix products: 15.5 us -> 0 us
  other arithmetic: 6.56 us -> 0 us
    pallas_call x0 -> x2, Pallas kernels: none -> 114 us  [the longest x1 112 us: per_device(): pl.pallas_call(functools.partial(gather_kernel, n_dx), out_shape=(pltpu.V...]
    ppermute x8 -> x0, waiting for transfers between devices: 79.2 us -> none  [from_partner(): lax.ppermute(value, axis, [(i, i ^ 1 << stride) for i in range(lax.axis_s...]
    ppermute x8 -> x0, starting transfers between devices: 17.3 us -> none  [from_partner(): lax.ppermute(value, axis, [(i, i ^ 1 << stride) for i in range(lax.axis_s...]
    dot_general x15 -> x0, matrix products: 15.5 us -> none  [the longest x5 5.56 us: transposed(): lax.dot_general(coeffs, images, (((0,), (0,)), ((), ())), preferred_eleme...]
    mul x2 -> x0, other arithmetic: 4.31 us -> none  [finish(): inverse * (grads - unit * jnp.sum(unit * grads, axis=-1, keepdims=True))]
    reduce_sum x2 -> x0, other arithmetic: 1.98 us -> none  [normalize(): jnp.sum(floats * floats, axis=-1, keepdims=True) + 1e-06]
  transfers between devices with their start and end apart: 8 -> 0, of which waited for: 3 -> 0; matrix products, arithmetic and copies ran while one was open for 13% -> 0% of each run, Pallas kernels for 0% -> 0%
where the time goes in v1:
time: 116 us
  Pallas kernels  114 us (98%)
  between operations  2.09 us (2%)
    pallas_call x1, Pallas kernels, per_device(): pl.pallas_call(functools.partial(gather_kernel, n_dx), out_shape=(pltpu.V...  112 us

profile of v1, /device:TPU:38, one launch (start us, length us, event | category | flops | bytes accessed | tf_op | source)
XLA Modules:
  0.0 116.2 jit_solution(3313373186991305691)
XLA Ops:
  1.9 111.9 %window_sums.1 = (f32[512,1152]{1,0:T(8,128)S(1)}, f32[512,1152]{1,0:T(8,128)S(1)}, bf16[2,512,1152]{2,1,0:T(8,128)(2,1)S(1)}, f32[2,512,1]{2,1,0:T(8,128)S(1)}) custom-call(bf16[512,1152]{1,0:T(8,128)(2,1)} %img.1, bf16[512,1152]{1,0:T(8,128)(2,1)} %txt.1, f32[1]{0:T(128)S(6)} %copy.6.scale_ref, f32[1]{0:T(128)S(6)} %copy.7.bias_ref), custom_call_target="tpu_custom_call" | custom-call | tf_op jit(solution)/shard_map/window_sums/pallas_call | solution.py:163
  113.8 2.2 %window_finish.1 = (f32[512,1152]{1,0:T(8,128)}, f32[512,1152]{1,0:T(8,128)}) custom-call(f32[512,1152]{1,0:T(8,128)S(1)} %get-tuple-element.6.grad_img, f32[512,1152]{1,0:T(8,128)S(1)} %get-tuple-element.7.sum_txt, bf16[2,512,1152]{2,1,0:T(8,128)(2,1)S(1)} %get-tuple-element.8.raw, f32[2,512,1]{2,1,0:T(8,128)S(1)} %get-tuple-element.9.inv), custom_call_target="tpu_custom_call" | custom-call | tf_op jit(solution)/shard_map/window_finish/pallas_call | solution.py:188

commit v2 on v1

v2 whole, which is shorter than its diff:
```python
import functools

import jax
import jax.numpy as jnp
from jax import lax
from jax.experimental import pallas as pl
from jax.experimental.pallas import tpu as pltpu
from jax.sharding import PartitionSpec as P

ROWS = 512
E = 1152
STEP = 256
FINISH_ROWS = 128
LAST_ROWS = 128
IMG, TXT = 0, 1
CORE, Y, X = 0, 1, 2
VMEM_LIMIT = 32 * 2**20
LIGHT = pl.CostEstimate(flops=1000, bytes_accessed=1000, transcendentals=0)


def flipped(index, bit):
    return jnp.where(lax.rem(index // bit, 2) == 1, index - bit, index + bit)


def projected(grads, raw, inverse):
    units = raw.astype(jnp.float32) * inverse
    return inverse * (grads - units * jnp.sum(units * grads, axis=-1, keepdims=True))


def unit_rows(values):
    floats = values.astype(jnp.float32)
    inverse = lax.rsqrt(jnp.sum(floats * floats, axis=-1, keepdims=True) + 1e-06)
    return floats * inverse, inverse


def tile(unit, scale, bias, others, row, diagonal=None):
    logits = scale * lax.dot_general(
        unit[pl.ds(row, STEP), :], others, (((1,), (1,)), ((), ())), preferred_element_type=jnp.float32
    ) + bias
    if diagonal is None:
        coeffs = jax.nn.sigmoid(logits)
    else:
        first = row + lax.broadcasted_iota(jnp.int32, logits.shape, 0)
        second = diagonal + lax.broadcasted_iota(jnp.int32, logits.shape, 1)
        signs = jnp.where(first == second, jnp.float32(1.0), jnp.float32(-1.0))
        coeffs = -signs * jax.nn.sigmoid(-signs * logits)
    return jnp.dot((scale * coeffs).astype(jnp.bfloat16), others, preferred_element_type=jnp.float32)


def add_tiles(sums, unit, scale, bias, far):
    count = STEP if far.shape[0] % STEP == 0 else 128

    @pl.loop(0, far.shape[0] // count)
    def _(step):
        others = unit_rows(far[pl.ds(step * count, count), :])[0].astype(jnp.bfloat16)
        for row in range(0, ROWS, STEP):
            sums[row : row + STEP, :] += tile(unit, scale, bias, others, row)


def near_kernel(img, txt, scale_ref, bias_ref, sum_img, sum_txt, raw, unit, inv, far, load_sem, send_sem, recv_sem):
    dx, dy = lax.axis_index("dx"), lax.axis_index("dy")
    partners = ((flipped(dx, 1), dy), (dx, flipped(dy, 1)), (flipped(dx, 2), dy))
    scale, bias = scale_ref[0], bias_ref[0]
    blocks = (img, txt)
    sums = (sum_img, sum_txt)

    loads = [pltpu.make_async_copy(blocks[kind], raw.at[kind], load_sem.at[kind]) for kind in (IMG, TXT)]
    for load in loads:
        load.start()

    barrier = pltpu.get_barrier_semaphore()
    for partner in partners:
        pl.semaphore_signal(barrier, inc=1, device_id=partner, device_id_type=pl.DeviceIdType.MESH)
    pl.semaphore_wait(barrier, 3)

    copies = {}
    for kind in (TXT, IMG):
        for way in (Y, X, CORE):
            copies[way, kind] = pltpu.make_async_remote_copy(
                src_ref=blocks[kind],
                dst_ref=far.at[way, kind],
                send_sem=send_sem.at[way, kind],
                recv_sem=recv_sem.at[way, kind],
                device_id=partners[way],
                device_id_type=pl.DeviceIdType.MESH,
            )
            copies[way, kind].start()

    for load in loads:
        load.wait()

    @pl.loop(0, ROWS // 128)
    def _(step):
        rows = pl.ds(step * 128, 128)
        for kind in (IMG, TXT):
            units, inverse = unit_rows(raw[kind, rows, :])
            unit[kind, rows, :] = units.astype(jnp.bfloat16)
            inv[kind, rows, :] = inverse

    for kind in (TXT, IMG):
        mine = 1 - kind
        for row in range(0, ROWS, STEP):
            rows = slice(row, row + STEP)
            sums[mine][rows, :] = tile(unit.at[mine], scale, bias, unit[kind, 0:STEP, :], row, 0)
            sums[mine][rows, :] += tile(unit.at[mine], scale, bias, unit[kind, STEP:ROWS, :], row, STEP)

    for way, kind in ((CORE, TXT), (CORE, IMG), (Y, TXT), (X, TXT), (Y, IMG), (X, IMG)):
        copies[way, kind].wait_recv()
        add_tiles(sums[1 - kind], unit.at[1 - kind], scale, bias, far.at[way, kind])

    for copy in copies.values():
        copy.wait_send()


def far_kernel(scale_ref, bias_ref, unit, far, sums_in, sums):
    add_tiles(sums, unit.at[TXT], scale_ref[0], bias_ref[0], far)


def closing_kernel(mine, scale_ref, bias_ref, unit, raw, inv, far, sums, out, grads, sem):
    scale, bias = scale_ref[0], bias_ref[0]
    if far.shape[0] > STEP:
        add_tiles(sums, unit.at[mine], scale, bias, far.at[0 : far.shape[0] - STEP])
        far = far.at[far.shape[0] - STEP : far.shape[0]]
    others = unit_rows(far[...])[0].astype(jnp.bfloat16)
    copies = []
    for row in range(0, ROWS, STEP):
        grads[row : row + STEP, :] = sums[row : row + STEP, :] + tile(unit.at[mine], scale, bias, others, row)
        for first in range(row, row + STEP, FINISH_ROWS):
            rows = pl.ds(first, FINISH_ROWS)
            grads[rows, :] = projected(grads[rows, :], raw[mine, rows, :], inv[mine, rows, :])
            copies.append(pltpu.make_async_copy(grads.at[rows], out.at[rows], sem.at[first // FINISH_ROWS]))
            copies[-1].start()
    for copy in copies:
        copy.wait()


def per_device(n_dx, img_emb, txt_emb, logit_scale, logit_bias):
    vmem = pl.BlockSpec(memory_space=pltpu.VMEM)
    smem = pl.BlockSpec(memory_space=pltpu.SMEM)
    params = pltpu.CompilerParams(vmem_limit_bytes=VMEM_LIMIT)
    scalars = (logit_scale, logit_bias)
    sum_shape = pltpu.VMEM((ROWS, E), jnp.float32)

    def across(value):
        half = n_dx // 2
        return lax.ppermute(value, "dx", [(i, i ^ half) for i in range(n_dx)])

    far_txt = across(txt_emb)
    far_img = across(img_emb[: ROWS - LAST_ROWS])
    far_last = across(img_emb[ROWS - LAST_ROWS :])

    hbm = [pltpu.with_memory_space_constraint(value, pltpu.HBM) for value in (img_emb, txt_emb)]
    sum_img, sum_txt, raw, unit, inv = pl.pallas_call(
        near_kernel,
        out_shape=(
            sum_shape,
            sum_shape,
            pltpu.VMEM((2, ROWS, E), jnp.bfloat16),
            pltpu.VMEM((2, ROWS, E), jnp.bfloat16),
            pltpu.VMEM((2, ROWS, 1), jnp.float32),
        ),
        in_specs=[pl.BlockSpec(memory_space=pltpu.HBM)] * 2 + [smem] * 2,
        out_specs=[vmem] * 5,
        scratch_shapes=[
            pltpu.VMEM((3, 2, ROWS, E), jnp.bfloat16),
            pltpu.SemaphoreType.DMA((2,)),
            pltpu.SemaphoreType.DMA((3, 2)),
            pltpu.SemaphoreType.DMA((3, 2)),
        ],
        compiler_params=pltpu.CompilerParams(collective_id=0, has_side_effects=True, vmem_limit_bytes=VMEM_LIMIT),
        cost_estimate=LIGHT,
        name="near_tiles",
    )(*hbm, *scalars)

    def closing(mine, far, sums, name):
        inputs = [pltpu.with_memory_space_constraint(value, pltpu.VMEM) for value in (unit, raw, inv, far, sums)]
        return pl.pallas_call(
            functools.partial(closing_kernel, mine),
            out_shape=jax.ShapeDtypeStruct((ROWS, E), jnp.float32),
            in_specs=[smem] * 2 + [vmem] * 5,
            out_specs=pl.BlockSpec(memory_space=pl.ANY),
            scratch_shapes=[
                pltpu.VMEM((ROWS, E), jnp.float32),
                pltpu.SemaphoreType.DMA((ROWS // FINISH_ROWS,)),
            ],
            compiler_params=params,
            cost_estimate=LIGHT,
            name=name,
        )(*scalars, *inputs)

    grad_img = closing(IMG, far_txt, sum_img, "close_img")
    grad_img, sum_txt = lax.optimization_barrier((grad_img, sum_txt))
    inputs = [pltpu.with_memory_space_constraint(value, pltpu.VMEM) for value in (unit, far_img, sum_txt)]
    sum_txt = pl.pallas_call(
        far_kernel,
        out_shape=sum_shape,
        in_specs=[smem] * 2 + [vmem] * 3,
        out_specs=vmem,
        input_output_aliases={4: 0},
        compiler_params=params,
        cost_estimate=LIGHT,
        name="far_img_tiles",
    )(*scalars, *inputs)
    grad_txt = closing(TXT, far_last, sum_txt, "close_txt")
    return grad_img, grad_txt


def solution(mesh):
    return jax.shard_map(
        functools.partial(per_device, mesh.shape["dx"]),
        mesh=mesh,
        in_specs=(P(("dx", "dy"), None), P(("dx", "dy"), None), P(), P()),
        out_specs=(P(("dx", "dy"), None), P(("dx", "dy"), None)),
        check_vma=False,
    )
```

time: 116 us -> 112 us (0.966)
  Pallas kernels: 114 us -> 71.5 us
  waiting for transfers between devices: 0 us -> 23.9 us
  starting transfers between devices: 0 us -> 12.5 us
  local copies, waits for them, and re-layouts: 0 us -> 2.22 us
    pallas_call x2 -> x4, Pallas kernels: 114 us -> 71.5 us  [the longest x1 61.3 us: per_device(): pl.pallas_call(near_kernel, out_shape=(sum_shape, sum_shape, pltpu.VMEM((...]
    ppermute x0 -> x3, waiting for transfers between devices: none -> 23.9 us  [across(): return lax.ppermute(value, 'dx', [(i, i ^ half) for i in range(n_dx)])]
    ppermute x0 -> x3, starting transfers between devices: none -> 12.5 us  [across(): return lax.ppermute(value, 'dx', [(i, i ^ half) for i in range(n_dx)])]
    slice x0 -> x2, local copies, waits for them, and re-layouts: none -> 2.22 us  [the longest x1 1.23 us: per_device(): far_img = across(img_emb[:ROWS - LAST_ROWS])]
  transfers between devices with their start and end apart: 0 -> 3, of which waited for: 0 -> 2; matrix products, arithmetic and copies ran while one was open for 0% -> 2% of each run, Pallas kernels for 0% -> 61%
where the time goes in v2:
time: 112 us
  Pallas kernels  71.5 us (64%)
  waiting for transfers between devices  23.9 us (21%)
  starting transfers between devices  12.5 us (11%)
  local copies, waits for them, and re-layouts  2.22 us (2%)
  between operations  2.13 us (2%)
    pallas_call x1, Pallas kernels, per_device(): pl.pallas_call(near_kernel, out_shape=(sum_shape, sum_shape, pltpu.VMEM((...  61.3 us
    ppermute x3, waiting for transfers between devices, across(): return lax.ppermute(value, 'dx', [(i, i ^ half) for i in range(n_dx)])  23.9 us
    ppermute x3, starting transfers between devices, across(): return lax.ppermute(value, 'dx', [(i, i ^ half) for i in range(n_dx)])  12.5 us
    pallas_call x2, Pallas kernels, closing(): pl.pallas_call(functools.partial(closing_kernel, mine), out_shape=jax.Sha...  6.26 us
    pallas_call x1, Pallas kernels, per_device(): pl.pallas_call(far_kernel, out_shape=sum_shape, in_specs=[smem] * 2 + [vm...  3.91 us
  transfers between devices with their start and end apart: 3, of which 2 were waited for; matrix products, arithmetic and copies ran while one was open for 2% of the time, Pallas kernels for 61%

profile of v2, /device:TPU:38, one launch (start us, length us, event | category | flops | bytes accessed | tf_op | source)
XLA Modules:
  0.0 112.3 jit_solution(14409839078866812743)
XLA Ops:
  0.6 6.4 %collective-permute-start = (bf16[512,1152]{1,0:T(8,128)(2,1)}, bf16[512,1152]{1,0:T(8,128)(2,1)S(1)}, u32[]{:S(2)}, u32[]{:S(2)}) collective-permute-start(bf16[512,1152]{1,0:T(8,128)(2,1)} %txt.1), channel_id=1, source_target_pairs={{0,128},{8,136},{16,144},{24,152},{32,160},{40,168},{48,176},{56,1... | collective-permute-start | bytes 3538952 | tf_op jit(solution)/shard_map/ppermute | solution.py:146
  7.0 1.2 %slice.7 = bf16[384,1152]{1,0:T(8,128)(2,1)S(1)} slice(bf16[512,1152]{1,0:T(8,128)(2,1)} %img.1), slice={[0:384], [0:1152]} | slice | bytes 1769472 | tf_op jit(solution)/shard_map/slice | solution.py:149
  8.2 0.1 collective-permute-start.2
  8.3 1.0 slice.6
  9.3 6.0 %collective-permute-start.1 = (bf16[128,1152]{1,0:T(8,128)(2,1)S(1)}, bf16[128,1152]{1,0:T(8,128)(2,1)S(1)}, u32[]{:S(2)}, u32[]{:S(2)}) collective-permute-start(bf16[128,1152]{1,0:T(8,128)(2,1)S(1)} %slice.6), channel_id=1, source_target_pairs={{0,128},{8,136},{16,144},{24,152},{32,160},{40,168},{48,176},{56,1... | collective-permute-start | bytes 884744 | tf_op jit(solution)/shard_map/ppermute | solution.py:146
  16.6 61.3 %near_tiles.1 = (f32[512,1152]{1,0:T(8,128)S(1)}, f32[512,1152]{1,0:T(8,128)S(1)}, bf16[2,512,1152]{2,1,0:T(8,128)(2,1)S(1)}, bf16[2,512,1152]{2,1,0:T(8,128)(2,1)S(1)}, f32[2,512,1]{2,1,0:T(8,128)S(1)}) custom-call(bf16[512,1152]{1,0:T(8,128)(2,1)} %img.1, bf16[512,1152]{1,0:T(8,128)(2,1)} %txt.1, f32[1]{0:T(128)S(6)} %copy.8.scale_ref, f32[1]{0:T(128)S(6)} %copy.9.bias_ref), custom_call_target="tpu_custom_call" | custom-call | flops 1000 | bytes 1000 | tf_op jit(solution)/shard_map/near_tiles/pallas_call | solution.py:153
  78.0 0.0 collective-permute-done.far
  78.0 3.7 %close_img.1 = f32[512,1152]{1,0:T(8,128)} custom-call(f32[1]{0:T(128)S(6)} %copy.8.scale_ref, f32[1]{0:T(128)S(6)} %copy.9.bias_ref, bf16[2,512,1152]{2,1,0:T(8,128)(2,1)S(1)} %get-tuple-element.9.unit, bf16[2,512,1152]{2,1,0:T(8,128)(2,1)S(1)} %get-tuple-element.10.raw, f32[2,512,1]{2,1,0:T(8,128)S(1)} %get-tuple-element.11.inv, ...), custom_call_target="tpu_custom_call" | custom-call | flops 1000 | bytes 1000 | tf_op jit(solution)/shard_map/close_img/pallas_call | solution.py:177
  81.7 22.4 %collective-permute-done.2.far = bf16[384,1152]{1,0:T(8,128)(2,1)S(1)} collective-permute-done((bf16[384,1152]{1,0:T(8,128)(2,1)S(1)}, bf16[384,1152]{1,0:T(8,128)(2,1)S(1)}, u32[]{:S(2)}, u32[]{:S(2)}) %collective-permute-start.2) | collective-permute-done | bytes 884768 | tf_op jit(solution)/shard_map/ppermute | solution.py:146
  104.0 3.9 %far_img_tiles.1.sums = f32[512,1152]{1,0:T(8,128)S(1)} custom-call(f32[1]{0:T(128)S(6)} %copy.8.scale_ref, f32[1]{0:T(128)S(6)} %copy.9.bias_ref, bf16[2,512,1152]{2,1,0:T(8,128)(2,1)S(1)} %get-tuple-element.9.unit, bf16[384,1152]{1,0:T(8,128)(2,1)S(1)} %collective-permute-done.2.far, ...), custom_call_target="tpu_custom_call", output_to_operand_aliasing={{}: (4, {})} | custom-call | flops 1000 | bytes 1000 | tf_op jit(solution)/shard_map/far_img_tiles/pallas_call | solution.py:194
  108.0 1.6 %collective-permute-done.1.far = bf16[128,1152]{1,0:T(8,128)(2,1)S(1)} collective-permute-done((bf16[128,1152]{1,0:T(8,128)(2,1)S(1)}, bf16[128,1152]{1,0:T(8,128)(2,1)S(1)}, u32[]{:S(2)}, u32[]{:S(2)}) %collective-permute-start.1) | collective-permute-done | bytes 294944 | tf_op jit(solution)/shard_map/ppermute | solution.py:146
  109.5 2.6 %close_txt.1 = f32[512,1152]{1,0:T(8,128)} custom-call(f32[1]{0:T(128)S(6)} %copy.8.scale_ref, f32[1]{0:T(128)S(6)} %copy.9.bias_ref, bf16[2,512,1152]{2,1,0:T(8,128)(2,1)S(1)} %get-tuple-element.9.unit, bf16[2,512,1152]{2,1,0:T(8,128)(2,1)S(1)} %get-tuple-element.10.raw, f32[2,512,1]{2,1,0:T(8,128)S(1)} %get-tuple-element.11.inv, ...), custom_call_target="tpu_custom_call" | custom-call | flops 1000 | bytes 1000 | tf_op jit(solution)/shard_map/close_txt/pallas_call | solution.py:177
Async XLA Ops:
  0.6 77.3 %collective-permute-start = (bf16[512,1152]{1,0:T(8,128)(2,1)}, bf16[512,1152]{1,0:T(8,128)(2,1)S(1)}, u32[]{:S(2)}, u32[]{:S(2)}) collective-permute-start(bf16[512,1152]{1,0:T(8,128)(2,1)} %txt.1), channel_id=1, source_target_pairs={{0,128},{8,136},{16,144},{24,152},{32,160},{40,168},{48,176},{56,1... | collective-permute-start | bytes 3538952 | tf_op jit(solution)/shard_map/ppermute | solution.py:146
  8.2 95.8 %collective-permute-start.2 = (bf16[384,1152]{1,0:T(8,128)(2,1)S(1)}, bf16[384,1152]{1,0:T(8,128)(2,1)S(1)}, u32[]{:S(2)}, u32[]{:S(2)}) collective-permute-start(bf16[384,1152]{1,0:T(8,128)(2,1)S(1)} %slice.7), channel_id=1, source_target_pairs={{0,128},{8,136},{16,144},{24,152},{32,160},{40,168},{48,176},{56,1... | collective-permute-start | bytes 2654216 | tf_op jit(solution)/shard_map/ppermute | solution.py:146
  9.3 100.2 %collective-permute-start.1 = (bf16[128,1152]{1,0:T(8,128)(2,1)S(1)}, bf16[128,1152]{1,0:T(8,128)(2,1)S(1)}, u32[]{:S(2)}, u32[]{:S(2)}) collective-permute-start(bf16[128,1152]{1,0:T(8,128)(2,1)S(1)} %slice.6), channel_id=1, source_target_pairs={{0,128},{8,136},{16,144},{24,152},{32,160},{40,168},{48,176},{56,1... | collective-permute-start | bytes 884744 | tf_op jit(solution)/shard_map/ppermute | solution.py:146

commit v3 on v2

--- a/solution.py
+++ b/solution.py
@@ -10,8 +10,9 @@
 ROWS = 512
 E = 1152
 STEP = 256
-FINISH_ROWS = 128
-LAST_ROWS = 128
+FINISH_ROWS = 64
+LAST_ROWS = 96
+CLOSE_CUTS = (0, 256, 448, 512)
 IMG, TXT = 0, 1
 CORE, Y, X = 0, 1, 2
 VMEM_LIMIT = 32 * 2**20
@@ -33,9 +34,9 @@
     return floats * inverse, inverse
 
 
-def tile(unit, scale, bias, others, row, diagonal=None):
+def tile(unit, scale, bias, others, row, diagonal=None, rows=STEP):
     logits = scale * lax.dot_general(
-        unit[pl.ds(row, STEP), :], others, (((1,), (1,)), ((), ())), preferred_element_type=jnp.float32
+        unit[pl.ds(row, rows), :], others, (((1,), (1,)), ((), ())), preferred_element_type=jnp.float32
     ) + bias
     if diagonal is None:
         coeffs = jax.nn.sigmoid(logits)
@@ -48,13 +49,15 @@
 
 
 def add_tiles(sums, unit, scale, bias, far):
-    count = STEP if far.shape[0] % STEP == 0 else 128
-
-    @pl.loop(0, far.shape[0] // count)
-    def _(step):
-        others = unit_rows(far[pl.ds(step * count, count), :])[0].astype(jnp.bfloat16)
+    def add(start, count):
+        others = unit_rows(far[pl.ds(start, count), :])[0].astype(jnp.bfloat16)
         for row in range(0, ROWS, STEP):
             sums[row : row + STEP, :] += tile(unit, scale, bias, others, row)
+
+    whole, rest = divmod(far.shape[0], STEP)
+    pl.loop(0, whole)(lambda step: add(step * STEP, STEP))
+    if rest:
+        add(whole * STEP, rest)
 
 
 def near_kernel(img, txt, scale_ref, bias_ref, sum_img, sum_txt, raw, unit, inv, far, load_sem, send_sem, recv_sem):
@@ -116,20 +119,25 @@
     add_tiles(sums, unit.at[TXT], scale_ref[0], bias_ref[0], far)
 
 
-def closing_kernel(mine, scale_ref, bias_ref, unit, raw, inv, far, sums, out, grads, sem):
+def closing_kernel(mine, scale_ref, bias_ref, unit, raw, inv, sums, far, out, grads, sem):
     scale, bias = scale_ref[0], bias_ref[0]
-    if far.shape[0] > STEP:
-        add_tiles(sums, unit.at[mine], scale, bias, far.at[0 : far.shape[0] - STEP])
-        far = far.at[far.shape[0] - STEP : far.shape[0]]
+    count = far.shape[0]
+    if count > STEP:
+        others = unit_rows(far[0 : count - STEP, :])[0].astype(jnp.bfloat16)
+        for row in range(0, ROWS, STEP):
+            grads[row : row + STEP, :] = sums[row : row + STEP, :] + tile(unit.at[mine], scale, bias, others, row)
+        sums = grads
+        far = far.at[count - STEP : count]
     others = unit_rows(far[...])[0].astype(jnp.bfloat16)
     copies = []
-    for row in range(0, ROWS, STEP):
-        grads[row : row + STEP, :] = sums[row : row + STEP, :] + tile(unit.at[mine], scale, bias, others, row)
-        for first in range(row, row + STEP, FINISH_ROWS):
-            rows = pl.ds(first, FINISH_ROWS)
+    for first, end in zip(CLOSE_CUTS, CLOSE_CUTS[1:]):
+        grads[first:end, :] = sums[first:end, :] + tile(unit.at[mine], scale, bias, others, first, rows=end - first)
+        for row in range(first, end, FINISH_ROWS):
+            rows = pl.ds(row, FINISH_ROWS)
             grads[rows, :] = projected(grads[rows, :], raw[mine, rows, :], inv[mine, rows, :])
-            copies.append(pltpu.make_async_copy(grads.at[rows], out.at[rows], sem.at[first // FINISH_ROWS]))
-            copies[-1].start()
+        part = pl.ds(first, end - first)
+        copies.append(pltpu.make_async_copy(grads.at[part], out.at[part], sem.at[len(copies)]))
+        copies[-1].start()
     for copy in copies:
         copy.wait()
 
@@ -173,7 +181,7 @@
     )(*hbm, *scalars)
 
     def closing(mine, far, sums, name):
-        inputs = [pltpu.with_memory_space_constraint(value, pltpu.VMEM) for value in (unit, raw, inv, far, sums)]
+        inputs = [pltpu.with_memory_space_constraint(value, pltpu.VMEM) for value in (unit, raw, inv, sums, far)]
         return pl.pallas_call(
             functools.partial(closing_kernel, mine),
             out_shape=jax.ShapeDtypeStruct((ROWS, E), jnp.float32),
@@ -181,7 +189,7 @@
             out_specs=pl.BlockSpec(memory_space=pl.ANY),
             scratch_shapes=[
                 pltpu.VMEM((ROWS, E), jnp.float32),
-                pltpu.SemaphoreType.DMA((ROWS // FINISH_ROWS,)),
+                pltpu.SemaphoreType.DMA((len(CLOSE_CUTS) - 1,)),
             ],
             compiler_params=params,
             cost_estimate=LIGHT,

time: 112 us -> 112 us (level)
  Pallas kernels: 71.5 us -> 70.2 us
  waiting for transfers between devices: 23.9 us -> 25.1 us
    pallas_call x1, Pallas kernels: 3.91 us -> 2.55 us  [per_device(): pl.pallas_call(far_kernel, out_shape=sum_shape, in_specs=[smem] * 2 + [vm...]
    ppermute x3, waiting for transfers between devices: 23.9 us -> 25.1 us  [across(): return lax.ppermute(value, 'dx', [(i, i ^ half) for i in range(n_dx)])]
  transfers between devices with their start and end apart: 3 -> 3, of which waited for: 2 -> 2; matrix products, arithmetic and copies ran while one was open for 2% -> 2% of each run, Pallas kernels for 61% -> 60%
where the time goes in v3:
time: 112 us
  Pallas kernels  70.2 us (63%)
  waiting for transfers between devices  25.1 us (22%)
  starting transfers between devices  12.5 us (11%)
  local copies, waits for them, and re-layouts  2.22 us (2%)
  between operations  2.13 us (2%)
    pallas_call x1, Pallas kernels, per_device(): pl.pallas_call(near_kernel, out_shape=(sum_shape, sum_shape, pltpu.VMEM((...  61.3 us
    ppermute x3, waiting for transfers between devices, across(): return lax.ppermute(value, 'dx', [(i, i ^ half) for i in range(n_dx)])  25.1 us
    ppermute x3, starting transfers between devices, across(): return lax.ppermute(value, 'dx', [(i, i ^ half) for i in range(n_dx)])  12.5 us
    pallas_call x2, Pallas kernels, closing(): pl.pallas_call(functools.partial(closing_kernel, mine), out_shape=jax.Sha...  6.38 us
    pallas_call x1, Pallas kernels, per_device(): pl.pallas_call(far_kernel, out_shape=sum_shape, in_specs=[smem] * 2 + [vm...  2.55 us
  transfers between devices with their start and end apart: 3, of which 2 were waited for; matrix products, arithmetic and copies ran while one was open for 2% of the time, Pallas kernels for 60%

profile of v3, /device:TPU:38, one launch (start us, length us, event | category | flops | bytes accessed | tf_op | source)
XLA Modules:
  0.0 112.2 jit_solution(10951288452420174369)
XLA Ops:
  0.6 6.4 %collective-permute-start = (bf16[512,1152]{1,0:T(8,128)(2,1)}, bf16[512,1152]{1,0:T(8,128)(2,1)S(1)}, u32[]{:S(2)}, u32[]{:S(2)}) collective-permute-start(bf16[512,1152]{1,0:T(8,128)(2,1)} %txt.1), channel_id=1, source_target_pairs={{0,128},{8,136},{16,144},{24,152},{32,160},{40,168},{48,176},{56,1... | collective-permute-start | bytes 3538952 | tf_op jit(solution)/shard_map/ppermute | solution.py:154
  7.0 1.3 %slice.6 = bf16[416,1152]{1,0:T(8,128)(2,1)S(1)} slice(bf16[512,1152]{1,0:T(8,128)(2,1)} %img.1), slice={[0:416], [0:1152]} | slice | bytes 1916928 | tf_op jit(solution)/shard_map/slice | solution.py:157
  8.3 0.1 collective-permute-start.1
  8.4 1.0 slice.7
  9.3 6.0 %collective-permute-start.2 = (bf16[96,1152]{1,0:T(8,128)(2,1)S(1)}, bf16[96,1152]{1,0:T(8,128)(2,1)S(1)}, u32[]{:S(2)}, u32[]{:S(2)}) collective-permute-start(bf16[96,1152]{1,0:T(8,128)(2,1)S(1)} %slice.7), channel_id=1, source_target_pairs={{0,128},{8,136},{16,144},{24,152},{32,160},{40,168},{48,176},{56,1... | collective-permute-start | bytes 663560 | tf_op jit(solution)/shard_map/ppermute | solution.py:154
  16.6 61.3 %near_tiles.1 = (f32[512,1152]{1,0:T(8,128)S(1)}, f32[512,1152]{1,0:T(8,128)S(1)}, bf16[2,512,1152]{2,1,0:T(8,128)(2,1)S(1)}, bf16[2,512,1152]{2,1,0:T(8,128)(2,1)S(1)}, f32[2,512,1]{2,1,0:T(8,128)S(1)}) custom-call(bf16[512,1152]{1,0:T(8,128)(2,1)} %img.1, bf16[512,1152]{1,0:T(8,128)(2,1)} %txt.1, f32[1]{0:T(128)S(6)} %copy.8.scale_ref, f32[1]{0:T(128)S(6)} %copy.9.bias_ref), custom_call_target="tpu_custom_call" | custom-call | flops 1000 | bytes 1000 | tf_op jit(solution)/shard_map/near_tiles/pallas_call | solution.py:161
  78.0 0.0 collective-permute-done.far
  78.0 3.9 %close_img.1 = f32[512,1152]{1,0:T(8,128)} custom-call(f32[1]{0:T(128)S(6)} %copy.8.scale_ref, f32[1]{0:T(128)S(6)} %copy.9.bias_ref, bf16[2,512,1152]{2,1,0:T(8,128)(2,1)S(1)} %get-tuple-element.9.unit, bf16[2,512,1152]{2,1,0:T(8,128)(2,1)S(1)} %get-tuple-element.10.raw, f32[2,512,1]{2,1,0:T(8,128)S(1)} %get-tuple-element.11.inv, ...), custom_call_target="tpu_custom_call" | custom-call | flops 1000 | bytes 1000 | tf_op jit(solution)/shard_map/close_img/pallas_call | solution.py:185
  81.9 23.8 %collective-permute-done.1.far = bf16[416,1152]{1,0:T(8,128)(2,1)S(1)} collective-permute-done((bf16[416,1152]{1,0:T(8,128)(2,1)S(1)}, bf16[416,1152]{1,0:T(8,128)(2,1)S(1)}, u32[]{:S(2)}, u32[]{:S(2)}) %collective-permute-start.1) | collective-permute-done | bytes 958496 | tf_op jit(solution)/shard_map/ppermute | solution.py:154
  105.6 2.5 %far_img_tiles.1.sums = f32[512,1152]{1,0:T(8,128)S(1)} custom-call(f32[1]{0:T(128)S(6)} %copy.8.scale_ref, f32[1]{0:T(128)S(6)} %copy.9.bias_ref, bf16[2,512,1152]{2,1,0:T(8,128)(2,1)S(1)} %get-tuple-element.9.unit, bf16[416,1152]{1,0:T(8,128)(2,1)S(1)} %collective-permute-done.1.far, ...), custom_call_target="tpu_custom_call", output_to_operand_aliasing={{}: (4, {})} | custom-call | flops 1000 | bytes 1000 | tf_op jit(solution)/shard_map/far_img_tiles/pallas_call | solution.py:202
  108.2 1.4 %collective-permute-done.2.far = bf16[96,1152]{1,0:T(8,128)(2,1)S(1)} collective-permute-done((bf16[96,1152]{1,0:T(8,128)(2,1)S(1)}, bf16[96,1152]{1,0:T(8,128)(2,1)S(1)}, u32[]{:S(2)}, u32[]{:S(2)}) %collective-permute-start.2) | collective-permute-done | bytes 221216 | tf_op jit(solution)/shard_map/ppermute | solution.py:154
  109.5 2.5 %close_txt.1 = f32[512,1152]{1,0:T(8,128)} custom-call(f32[1]{0:T(128)S(6)} %copy.8.scale_ref, f32[1]{0:T(128)S(6)} %copy.9.bias_ref, bf16[2,512,1152]{2,1,0:T(8,128)(2,1)S(1)} %get-tuple-element.9.unit, bf16[2,512,1152]{2,1,0:T(8,128)(2,1)S(1)} %get-tuple-element.10.raw, f32[2,512,1]{2,1,0:T(8,128)S(1)} %get-tuple-element.11.inv, ...), custom_call_target="tpu_custom_call" | custom-call | flops 1000 | bytes 1000 | tf_op jit(solution)/shard_map/close_txt/pallas_call | solution.py:185
Async XLA Ops:
  0.6 77.3 %collective-permute-start = (bf16[512,1152]{1,0:T(8,128)(2,1)}, bf16[512,1152]{1,0:T(8,128)(2,1)S(1)}, u32[]{:S(2)}, u32[]{:S(2)}) collective-permute-start(bf16[512,1152]{1,0:T(8,128)(2,1)} %txt.1), channel_id=1, source_target_pairs={{0,128},{8,136},{16,144},{24,152},{32,160},{40,168},{48,176},{56,1... | collective-permute-start | bytes 3538952 | tf_op jit(solution)/shard_map/ppermute | solution.py:154
  8.3 97.4 %collective-permute-start.1 = (bf16[416,1152]{1,0:T(8,128)(2,1)S(1)}, bf16[416,1152]{1,0:T(8,128)(2,1)S(1)}, u32[]{:S(2)}, u32[]{:S(2)}) collective-permute-start(bf16[416,1152]{1,0:T(8,128)(2,1)S(1)} %slice.6), channel_id=1, source_target_pairs={{0,128},{8,136},{16,144},{24,152},{32,160},{40,168},{48,176},{56,1... | collective-permute-start | bytes 2875400 | tf_op jit(solution)/shard_map/ppermute | solution.py:154
  9.3 100.2 %collective-permute-start.2 = (bf16[96,1152]{1,0:T(8,128)(2,1)S(1)}, bf16[96,1152]{1,0:T(8,128)(2,1)S(1)}, u32[]{:S(2)}, u32[]{:S(2)}) collective-permute-start(bf16[96,1152]{1,0:T(8,128)(2,1)S(1)} %slice.7), channel_id=1, source_target_pairs={{0,128},{8,136},{16,144},{24,152},{32,160},{40,168},{48,176},{56,1... | collective-permute-start | bytes 663560 | tf_op jit(solution)/shard_map/ppermute | solution.py:154

commit v4 on v3

--- a/solution.py
+++ b/solution.py
@@ -11,7 +11,7 @@
 E = 1152
 STEP = 256
 FINISH_ROWS = 64
-LAST_ROWS = 96
+LAST_ROWS = 128
 CLOSE_CUTS = (0, 256, 448, 512)
 IMG, TXT = 0, 1
 CORE, Y, X = 0, 1, 2
@@ -128,10 +128,17 @@
             grads[row : row + STEP, :] = sums[row : row + STEP, :] + tile(unit.at[mine], scale, bias, others, row)
         sums = grads
         far = far.at[count - STEP : count]
-    others = unit_rows(far[...])[0].astype(jnp.bfloat16)
+    others = far[...]
+    inverse = unit_rows(others)[1]
+    inverse = jnp.broadcast_to(inverse, (inverse.shape[0], 128)).T[0:1, :]
     copies = []
     for first, end in zip(CLOSE_CUTS, CLOSE_CUTS[1:]):
-        grads[first:end, :] = sums[first:end, :] + tile(unit.at[mine], scale, bias, others, first, rows=end - first)
+        dots = lax.dot_general(
+            unit[mine, first:end, :], others, (((1,), (1,)), ((), ())), preferred_element_type=jnp.float32
+        )
+        coeffs = scale * jax.nn.sigmoid(dots * (scale * inverse) + bias) * inverse
+        more = jnp.dot(coeffs.astype(jnp.bfloat16), others, preferred_element_type=jnp.float32)
+        grads[first:end, :] = sums[first:end, :] + more
         for row in range(first, end, FINISH_ROWS):
             rows = pl.ds(row, FINISH_ROWS)
             grads[rows, :] = projected(grads[rows, :], raw[mine, rows, :], inv[mine, rows, :])

time: 112 us -> 112 us (level)
  transfers between devices with their start and end apart: 3 -> 3, of which waited for: 2 -> 2; matrix products, arithmetic and copies ran while one was open for 2% -> 2% of each run, Pallas kernels for 60% -> 61%
where the time goes in v4:
time: 112 us
  Pallas kernels  70.3 us (63%)
  waiting for transfers between devices  25 us (22%)
  starting transfers between devices  12.5 us (11%)
  local copies, waits for them, and re-layouts  2.22 us (2%)
  between operations  2.13 us (2%)
    pallas_call x1, Pallas kernels, per_device(): pl.pallas_call(near_kernel, out_shape=(sum_shape, sum_shape, pltpu.VMEM((...  61.3 us
    ppermute x3, waiting for transfers between devices, across(): return lax.ppermute(value, 'dx', [(i, i ^ half) for i in range(n_dx)])  25 us
    ppermute x3, starting transfers between devices, across(): return lax.ppermute(value, 'dx', [(i, i ^ half) for i in range(n_dx)])  12.5 us
    pallas_call x2, Pallas kernels, closing(): pl.pallas_call(functools.partial(closing_kernel, mine), out_shape=jax.Sha...  6.34 us
    pallas_call x1, Pallas kernels, per_device(): pl.pallas_call(far_kernel, out_shape=sum_shape, in_specs=[smem] * 2 + [vm...  2.65 us
  transfers between devices with their start and end apart: 3, of which 2 were waited for; matrix products, arithmetic and copies ran while one was open for 2% of the time, Pallas kernels for 61%

profile of v4, /device:TPU:38, one launch (start us, length us, event | category | flops | bytes accessed | tf_op | source)
XLA Modules:
  0.0 112.1 jit_solution(8409428208322692723)
XLA Ops:
  0.6 6.4 %collective-permute-start = (bf16[512,1152]{1,0:T(8,128)(2,1)}, bf16[512,1152]{1,0:T(8,128)(2,1)S(1)}, u32[]{:S(2)}, u32[]{:S(2)}) collective-permute-start(bf16[512,1152]{1,0:T(8,128)(2,1)} %txt.1), channel_id=1, source_target_pairs={{0,128},{8,136},{16,144},{24,152},{32,160},{40,168},{48,176},{56,1... | collective-permute-start | bytes 3538952 | tf_op jit(solution)/shard_map/ppermute | solution.py:161
  7.0 1.2 %slice.6 = bf16[384,1152]{1,0:T(8,128)(2,1)S(1)} slice(bf16[512,1152]{1,0:T(8,128)(2,1)} %img.1), slice={[0:384], [0:1152]} | slice | bytes 1769472 | tf_op jit(solution)/shard_map/slice | solution.py:164
  8.2 0.1 collective-permute-start.1
  8.3 1.0 slice.7
  9.3 6.0 %collective-permute-start.2 = (bf16[128,1152]{1,0:T(8,128)(2,1)S(1)}, bf16[128,1152]{1,0:T(8,128)(2,1)S(1)}, u32[]{:S(2)}, u32[]{:S(2)}) collective-permute-start(bf16[128,1152]{1,0:T(8,128)(2,1)S(1)} %slice.7), channel_id=1, source_target_pairs={{0,128},{8,136},{16,144},{24,152},{32,160},{40,168},{48,176},{56,1... | collective-permute-start | bytes 884744 | tf_op jit(solution)/shard_map/ppermute | solution.py:161
  16.6 61.3 %near_tiles.1 = (f32[512,1152]{1,0:T(8,128)S(1)}, f32[512,1152]{1,0:T(8,128)S(1)}, bf16[2,512,1152]{2,1,0:T(8,128)(2,1)S(1)}, bf16[2,512,1152]{2,1,0:T(8,128)(2,1)S(1)}, f32[2,512,1]{2,1,0:T(8,128)S(1)}) custom-call(bf16[512,1152]{1,0:T(8,128)(2,1)} %img.1, bf16[512,1152]{1,0:T(8,128)(2,1)} %txt.1, f32[1]{0:T(128)S(6)} %copy.8.scale_ref, f32[1]{0:T(128)S(6)} %copy.9.bias_ref), custom_call_target="tpu_custom_call" | custom-call | flops 1000 | bytes 1000 | tf_op jit(solution)/shard_map/near_tiles/pallas_call | solution.py:168
  78.0 0.0 collective-permute-done.far
  78.0 3.9 %close_img.1 = f32[512,1152]{1,0:T(8,128)} custom-call(f32[1]{0:T(128)S(6)} %copy.8.scale_ref, f32[1]{0:T(128)S(6)} %copy.9.bias_ref, bf16[2,512,1152]{2,1,0:T(8,128)(2,1)S(1)} %get-tuple-element.9.unit, bf16[2,512,1152]{2,1,0:T(8,128)(2,1)S(1)} %get-tuple-element.10.raw, f32[2,512,1]{2,1,0:T(8,128)S(1)} %get-tuple-element.11.inv, ...), custom_call_target="tpu_custom_call" | custom-call | flops 1000 | bytes 1000 | tf_op jit(solution)/shard_map/close_img/pallas_call | solution.py:192
  81.9 22.1 %collective-permute-done.1.far = bf16[384,1152]{1,0:T(8,128)(2,1)S(1)} collective-permute-done((bf16[384,1152]{1,0:T(8,128)(2,1)S(1)}, bf16[384,1152]{1,0:T(8,128)(2,1)S(1)}, u32[]{:S(2)}, u32[]{:S(2)}) %collective-permute-start.1) | collective-permute-done | bytes 884768 | tf_op jit(solution)/shard_map/ppermute | solution.py:161
  104.0 2.6 %far_img_tiles.1.sums = f32[512,1152]{1,0:T(8,128)S(1)} custom-call(f32[1]{0:T(128)S(6)} %copy.8.scale_ref, f32[1]{0:T(128)S(6)} %copy.9.bias_ref, bf16[2,512,1152]{2,1,0:T(8,128)(2,1)S(1)} %get-tuple-element.9.unit, bf16[384,1152]{1,0:T(8,128)(2,1)S(1)} %collective-permute-done.1.far, ...), custom_call_target="tpu_custom_call", output_to_operand_aliasing={{}: (4, {})} | custom-call | flops 1000 | bytes 1000 | tf_op jit(solution)/shard_map/far_img_tiles/pallas_call | solution.py:209
  106.7 2.8 %collective-permute-done.2.far = bf16[128,1152]{1,0:T(8,128)(2,1)S(1)} collective-permute-done((bf16[128,1152]{1,0:T(8,128)(2,1)S(1)}, bf16[128,1152]{1,0:T(8,128)(2,1)S(1)}, u32[]{:S(2)}, u32[]{:S(2)}) %collective-permute-start.2) | collective-permute-done | bytes 294944 | tf_op jit(solution)/shard_map/ppermute | solution.py:161
  109.5 2.4 %close_txt.1 = f32[512,1152]{1,0:T(8,128)} custom-call(f32[1]{0:T(128)S(6)} %copy.8.scale_ref, f32[1]{0:T(128)S(6)} %copy.9.bias_ref, bf16[2,512,1152]{2,1,0:T(8,128)(2,1)S(1)} %get-tuple-element.9.unit, bf16[2,512,1152]{2,1,0:T(8,128)(2,1)S(1)} %get-tuple-element.10.raw, f32[2,512,1]{2,1,0:T(8,128)S(1)} %get-tuple-element.11.inv, ...), custom_call_target="tpu_custom_call" | custom-call | flops 1000 | bytes 1000 | tf_op jit(solution)/shard_map/close_txt/pallas_call | solution.py:192
Async XLA Ops:
  0.6 77.3 %collective-permute-start = (bf16[512,1152]{1,0:T(8,128)(2,1)}, bf16[512,1152]{1,0:T(8,128)(2,1)S(1)}, u32[]{:S(2)}, u32[]{:S(2)}) collective-permute-start(bf16[512,1152]{1,0:T(8,128)(2,1)} %txt.1), channel_id=1, source_target_pairs={{0,128},{8,136},{16,144},{24,152},{32,160},{40,168},{48,176},{56,1... | collective-permute-start | bytes 3538952 | tf_op jit(solution)/shard_map/ppermute | solution.py:161
  8.2 95.8 %collective-permute-start.1 = (bf16[384,1152]{1,0:T(8,128)(2,1)S(1)}, bf16[384,1152]{1,0:T(8,128)(2,1)S(1)}, u32[]{:S(2)}, u32[]{:S(2)}) collective-permute-start(bf16[384,1152]{1,0:T(8,128)(2,1)S(1)} %slice.6), channel_id=1, source_target_pairs={{0,128},{8,136},{16,144},{24,152},{32,160},{40,168},{48,176},{56,1... | collective-permute-start | bytes 2654216 | tf_op jit(solution)/shard_map/ppermute | solution.py:161
  9.3 100.2 %collective-permute-start.2 = (bf16[128,1152]{1,0:T(8,128)(2,1)S(1)}, bf16[128,1152]{1,0:T(8,128)(2,1)S(1)}, u32[]{:S(2)}, u32[]{:S(2)}) collective-permute-start(bf16[128,1152]{1,0:T(8,128)(2,1)S(1)} %slice.7), channel_id=1, source_target_pairs={{0,128},{8,136},{16,144},{24,152},{32,160},{40,168},{48,176},{56,1... | collective-permute-start | bytes 884744 | tf_op jit(solution)/shard_map/ppermute | solution.py:161

commit v5 on v4

--- a/solution.py
+++ b/solution.py
@@ -11,7 +11,7 @@
 E = 1152
 STEP = 256
 FINISH_ROWS = 64
-LAST_ROWS = 128
+LAST_ROWS = 96
 CLOSE_CUTS = (0, 256, 448, 512)
 IMG, TXT = 0, 1
 CORE, Y, X = 0, 1, 2

time: 112 us -> 112 us (level)
  transfers between devices with their start and end apart: 3 -> 3, of which waited for: 2 -> 2; matrix products, arithmetic and copies ran while one was open for 2% -> 2% of each run, Pallas kernels for 61% -> 60%
where the time goes in v5:
time: 112 us
  Pallas kernels  70.2 us (63%)
  waiting for transfers between devices  25.1 us (22%)
  starting transfers between devices  12.5 us (11%)
  local copies, waits for them, and re-layouts  2.22 us (2%)
  between operations  2.13 us (2%)
    pallas_call x1, Pallas kernels, per_device(): pl.pallas_call(near_kernel, out_shape=(sum_shape, sum_shape, pltpu.VMEM((...  61.3 us
    ppermute x3, waiting for transfers between devices, across(): return lax.ppermute(value, 'dx', [(i, i ^ half) for i in range(n_dx)])  25.1 us
    ppermute x3, starting transfers between devices, across(): return lax.ppermute(value, 'dx', [(i, i ^ half) for i in range(n_dx)])  12.5 us
    pallas_call x2, Pallas kernels, closing(): pl.pallas_call(functools.partial(closing_kernel, mine), out_shape=jax.Sha...  6.33 us
    pallas_call x1, Pallas kernels, per_device(): pl.pallas_call(far_kernel, out_shape=sum_shape, in_specs=[smem] * 2 + [vm...  2.55 us
  transfers between devices with their start and end apart: 3, of which 2 were waited for; matrix products, arithmetic and copies ran while one was open for 2% of the time, Pallas kernels for 60%

profile of v5, /device:TPU:38, one launch (start us, length us, event | category | flops | bytes accessed | tf_op | source)
XLA Modules:
  0.0 112.1 jit_solution(14607622680451642824)
XLA Ops:
  0.6 6.4 %collective-permute-start = (bf16[512,1152]{1,0:T(8,128)(2,1)}, bf16[512,1152]{1,0:T(8,128)(2,1)S(1)}, u32[]{:S(2)}, u32[]{:S(2)}) collective-permute-start(bf16[512,1152]{1,0:T(8,128)(2,1)} %txt.1), channel_id=1, source_target_pairs={{0,128},{8,136},{16,144},{24,152},{32,160},{40,168},{48,176},{56,1... | collective-permute-start | bytes 3538952 | tf_op jit(solution)/shard_map/ppermute | solution.py:161
  7.0 1.3 %slice.6 = bf16[416,1152]{1,0:T(8,128)(2,1)S(1)} slice(bf16[512,1152]{1,0:T(8,128)(2,1)} %img.1), slice={[0:416], [0:1152]} | slice | bytes 1916928 | tf_op jit(solution)/shard_map/slice | solution.py:164
  8.3 0.1 collective-permute-start.1
  8.4 1.0 slice.7
  9.3 6.0 %collective-permute-start.2 = (bf16[96,1152]{1,0:T(8,128)(2,1)S(1)}, bf16[96,1152]{1,0:T(8,128)(2,1)S(1)}, u32[]{:S(2)}, u32[]{:S(2)}) collective-permute-start(bf16[96,1152]{1,0:T(8,128)(2,1)S(1)} %slice.7), channel_id=1, source_target_pairs={{0,128},{8,136},{16,144},{24,152},{32,160},{40,168},{48,176},{56,1... | collective-permute-start | bytes 663560 | tf_op jit(solution)/shard_map/ppermute | solution.py:161
  16.6 61.3 %near_tiles.1 = (f32[512,1152]{1,0:T(8,128)S(1)}, f32[512,1152]{1,0:T(8,128)S(1)}, bf16[2,512,1152]{2,1,0:T(8,128)(2,1)S(1)}, bf16[2,512,1152]{2,1,0:T(8,128)(2,1)S(1)}, f32[2,512,1]{2,1,0:T(8,128)S(1)}) custom-call(bf16[512,1152]{1,0:T(8,128)(2,1)} %img.1, bf16[512,1152]{1,0:T(8,128)(2,1)} %txt.1, f32[1]{0:T(128)S(6)} %copy.8.scale_ref, f32[1]{0:T(128)S(6)} %copy.9.bias_ref), custom_call_target="tpu_custom_call" | custom-call | flops 1000 | bytes 1000 | tf_op jit(solution)/shard_map/near_tiles/pallas_call | solution.py:168
  78.0 0.0 collective-permute-done.far
  78.0 3.9 %close_img.1 = f32[512,1152]{1,0:T(8,128)} custom-call(f32[1]{0:T(128)S(6)} %copy.8.scale_ref, f32[1]{0:T(128)S(6)} %copy.9.bias_ref, bf16[2,512,1152]{2,1,0:T(8,128)(2,1)S(1)} %get-tuple-element.9.unit, bf16[2,512,1152]{2,1,0:T(8,128)(2,1)S(1)} %get-tuple-element.10.raw, f32[2,512,1]{2,1,0:T(8,128)S(1)} %get-tuple-element.11.inv, ...), custom_call_target="tpu_custom_call" | custom-call | flops 1000 | bytes 1000 | tf_op jit(solution)/shard_map/close_img/pallas_call | solution.py:192
  81.9 23.7 %collective-permute-done.1.far = bf16[416,1152]{1,0:T(8,128)(2,1)S(1)} collective-permute-done((bf16[416,1152]{1,0:T(8,128)(2,1)S(1)}, bf16[416,1152]{1,0:T(8,128)(2,1)S(1)}, u32[]{:S(2)}, u32[]{:S(2)}) %collective-permute-start.1) | collective-permute-done | bytes 958496 | tf_op jit(solution)/shard_map/ppermute | solution.py:161
  105.6 2.5 %far_img_tiles.1.sums = f32[512,1152]{1,0:T(8,128)S(1)} custom-call(f32[1]{0:T(128)S(6)} %copy.8.scale_ref, f32[1]{0:T(128)S(6)} %copy.9.bias_ref, bf16[2,512,1152]{2,1,0:T(8,128)(2,1)S(1)} %get-tuple-element.9.unit, bf16[416,1152]{1,0:T(8,128)(2,1)S(1)} %collective-permute-done.1.far, ...), custom_call_target="tpu_custom_call", output_to_operand_aliasing={{}: (4, {})} | custom-call | flops 1000 | bytes 1000 | tf_op jit(solution)/shard_map/far_img_tiles/pallas_call | solution.py:209
  108.2 1.4 %collective-permute-done.2.far = bf16[96,1152]{1,0:T(8,128)(2,1)S(1)} collective-permute-done((bf16[96,1152]{1,0:T(8,128)(2,1)S(1)}, bf16[96,1152]{1,0:T(8,128)(2,1)S(1)}, u32[]{:S(2)}, u32[]{:S(2)}) %collective-permute-start.2) | collective-permute-done | bytes 221216 | tf_op jit(solution)/shard_map/ppermute | solution.py:161
  109.5 2.4 %close_txt.1 = f32[512,1152]{1,0:T(8,128)} custom-call(f32[1]{0:T(128)S(6)} %copy.8.scale_ref, f32[1]{0:T(128)S(6)} %copy.9.bias_ref, bf16[2,512,1152]{2,1,0:T(8,128)(2,1)S(1)} %get-tuple-element.9.unit, bf16[2,512,1152]{2,1,0:T(8,128)(2,1)S(1)} %get-tuple-element.10.raw, f32[2,512,1]{2,1,0:T(8,128)S(1)} %get-tuple-element.11.inv, ...), custom_call_target="tpu_custom_call" | custom-call | flops 1000 | bytes 1000 | tf_op jit(solution)/shard_map/close_txt/pallas_call | solution.py:192
Async XLA Ops:
  0.6 77.3 %collective-permute-start = (bf16[512,1152]{1,0:T(8,128)(2,1)}, bf16[512,1152]{1,0:T(8,128)(2,1)S(1)}, u32[]{:S(2)}, u32[]{:S(2)}) collective-permute-start(bf16[512,1152]{1,0:T(8,128)(2,1)} %txt.1), channel_id=1, source_target_pairs={{0,128},{8,136},{16,144},{24,152},{32,160},{40,168},{48,176},{56,1... | collective-permute-start | bytes 3538952 | tf_op jit(solution)/shard_map/ppermute | solution.py:161
  8.3 97.4 %collective-permute-start.1 = (bf16[416,1152]{1,0:T(8,128)(2,1)S(1)}, bf16[416,1152]{1,0:T(8,128)(2,1)S(1)}, u32[]{:S(2)}, u32[]{:S(2)}) collective-permute-start(bf16[416,1152]{1,0:T(8,128)(2,1)S(1)} %slice.6), channel_id=1, source_target_pairs={{0,128},{8,136},{16,144},{24,152},{32,160},{40,168},{48,176},{56,1... | collective-permute-start | bytes 2875400 | tf_op jit(solution)/shard_map/ppermute | solution.py:161
  9.3 100.2 %collective-permute-start.2 = (bf16[96,1152]{1,0:T(8,128)(2,1)S(1)}, bf16[96,1152]{1,0:T(8,128)(2,1)S(1)}, u32[]{:S(2)}, u32[]{:S(2)}) collective-permute-start(bf16[96,1152]{1,0:T(8,128)(2,1)S(1)} %slice.7), channel_id=1, source_target_pairs={{0,128},{8,136},{16,144},{24,152},{32,160},{40,168},{48,176},{56,1... | collective-permute-start | bytes 663560 | tf_op jit(solution)/shard_map/ppermute | solution.py:161
